TPU v7x, 1024 devices: a whole 4x8x16 slice. The times are simulated.
1024 devices in a mesh: row: 32 (over x, y), col: 32 (over z, core).
Axes of the slice: x: 4, y: 8, z: 16, core: 2. Of those that a mesh axis runs over, the one named last changes fastest.
Arguments:
- amp_cycle: float32 [4096, 64, 128], P(('row', 'col')), may hold values from -6 to 6
- cycle_ints: float32 [32768, 2, 64, 64], P(('row', 'col')), may hold values from -0.5 to 0.5
- cycle_refs: int32 [32768, 2], P(('row', 'col')), may hold values from 0 to 31, as said below
- wanted: int32 [1024, 32, 1], P(('row', 'col')), may hold values from 0 to 3, as said below
- cycle_dest: int32 [32768], P(('row', 'col')), may hold values from 0 to 1023, as said below
- ladder_ints: float32 [8192, 64, 64], P(('row', 'col')), may hold values from -0.5 to 0.5
- ladder_amps: float32 [8192, 64, 128], P(('row', 'col')), may hold values from -6 to 6
- ladder_int_ref: int32 [32768, 2], P(('row', 'col')), may hold values from 0 to 7
- ladder_amp_ref: int32 [32768, 2], P(('row', 'col')), may hold values from 0 to 7
Outputs:
- residual: float32 [32768, 64, 128], P(('row', 'col'))
Inputs may be any that keep to these rules, and one draw needn't show every extreme that they name: `cycle_refs`: within one device's cycle tiles, every value 0 to 31 appears exactly 32 * 2 / 32 times. For each device and each h, the 1 entries wanted[d, h, :] are distinct. Each device sends exactly 1 of its cycle tiles to each index of row (cycle_dest // 32), and within each column group every ladder tile receives exactly one cycle tile.
All inputs are finite; a program needn't handle non-finite values.
Results may differ from a plain program's by a relative error of at most 0.0003.
Values sent between devices are 32-bit elements; how exact they have to be, the bound alone decides.
A program may use at most 32 MiB of HBM per device.

v0:
```python
import jax
import jax.numpy as jnp
from jax import lax
from jax.sharding import PartitionSpec as P


def body(
    amp_cycle,
    cycle_ints,
    cycle_refs,
    wanted,
    cycle_dest,
    ladder_ints,
    ladder_amps,
    ladder_int_ref,
    ladder_amp_ref,
):
    highest = lax.Precision.HIGHEST
    col_count = lax.axis_size("col")
    row_count = lax.axis_size("row")
    held_count = amp_cycle.shape[0]
    tile_size = amp_cycle.shape[1]
    slab_size = amp_cycle.shape[2]
    wanted_here = wanted[0]
    gathered = lax.all_gather(amp_cycle, "col", axis=0, tiled=True)
    holders = jnp.arange(col_count, dtype=jnp.int32)[:, None]
    lookup = (holders * held_count + wanted_here).reshape(-1)
    sources = gathered[lookup[cycle_refs]]
    cycle_part = jnp.einsum("tsij,tsjk->tik", cycle_ints, sources, precision=highest)
    cycle_count = cycle_dest.shape[0]
    per_peer = cycle_count // row_count
    sorting = jnp.argsort(cycle_dest)
    outgoing = cycle_part[sorting].reshape(row_count, per_peer, tile_size, slab_size)
    slot_index = (
        (cycle_dest % cycle_count)[sorting].astype(jnp.float32).reshape(row_count, per_peer)
    )
    arrived, arrived_slot = (
        lax.all_to_all(outgoing, "row", split_axis=0, concat_axis=0, tiled=True),
        lax.all_to_all(slot_index, "row", split_axis=0, concat_axis=0, tiled=True),
    )
    placement = arrived_slot.reshape(-1).astype(jnp.int32)
    cycle_here = (
        jnp.zeros_like(cycle_part)
        .at[placement]
        .set(arrived.reshape(cycle_count, tile_size, slab_size))
    )
    ladder_tiles = ladder_ints[ladder_int_ref]
    ladder_sources = ladder_amps[ladder_amp_ref]
    ladder_sum = jnp.einsum("tmij,tmjk->tik", ladder_tiles, ladder_sources, precision=highest)
    return ladder_sum + cycle_here


def solution(mesh):
    placed = (
        P(("row", "col"), None, None),
        P(("row", "col"), None, None, None),
        P(("row", "col"), None),
        P(("row", "col"), None, None),
        P(("row", "col")),
        P(("row", "col"), None, None),
        P(("row", "col"), None, None),
        P(("row", "col"), None),
        P(("row", "col"), None),
    )
    return jax.shard_map(
        body, mesh=mesh, in_specs=placed, out_specs=P(("row", "col"), None, None), check_vma=False
    )
```

profile of v0, /device:TPU:8, one launch (start us, length us, event | category | flops | bytes accessed | tf_op | source)
XLA Modules:
  0.0 159.9 jit_solution(16246376321165850387)
XLA Ops:
  6.5 0.7 all-gather.2.cloned.1.call-update
  7.3 2.3 %sort.17 = (s32[32]{0:T(128)}, s32[32]{0:T(128)S(1)}) sort(s32[32]{0:T(128)} %param.13, s32[32]{0:T(128)S(1)} %iota.9), dimensions={0}, to_apply=%region_0.0 | sort | flops 160 | bytes 512 | tf_op jit(solution)/shard_map/jit(argsort)/sort | solution.py:32
  9.5 0.7 and_select_fusion
  10.2 0.7 gather_fusion.2
  10.9 0.7 copy.23
  11.6 16.5 %all-to-all-start = ((f32[32,1,1]{2,1,0:T(1,128)}), f32[32,1,1]{2,1,0:T(1,128)S(1)}, u32[]{:S(2)}, u32[]{:S(2)}) async-start(f32[32,1,1]{2,1,0:T(1,128)} %copy.23), calls=%async_computation | async-start | bytes 32768 | tf_op jit(solution)/shard_map/all_to_all | solution.py:39
  28.1 0.7 compare_select_fusion.1
  29.0 0.7 bitcast_add_fusion
  29.7 0.8 gather_fusion.3
  30.6 0.1 reshape.95
  30.7 65.0 %all-gather.2.cloned.1.call-done = f32[128,64,128]{2,1,0:T(8,128)} async-done(((f32[4,64,128]{2,1,0:T(8,128)}), f32[128,64,128]{2,1,0:T(8,128)}) %all-gather.2.cloned.1.call-update) | async-done | bytes 4194320 | tf_op jit(solution)/shard_map/all_gather | solution.py:25
  95.7 4.2 %gather_fusion.4 = f32[64,64,128]{2,1,0:T(8,128)} fusion(f32[128,64,128]{2,1,0:T(8,128)} %all-gather.2.cloned.1.call-done, s32[1024]{0:T(1024)S(1)} %pad_clamp_fusion), kind=kCustom, calls=%fused_computation.4 | custom fusion | bytes 4194560 | tf_op jit(solution)/shard_map/gather | solution.py:28
  99.9 3.7 %convolution_bitcast_fusion = f32[32,64,128]{2,1,0:T(8,128)S(1)} fusion(f32[32,2,64,128]{3,2,1,0:T(8,128)} %bitcast.33, f32[32,2,64,64]{3,2,1,0:T(8,128)S(1)} %copy-done), kind=kOutput, calls=%fused_computation.7 | convolution fusion | flops 402653184 | bytes 4194304 | tf_op jit(solution)/shard_map/tsij,tsjk->tik/dot_general | solution.py:29
  103.6 1.6 gather_fusion.5
  105.2 9.9 %all-to-all-start.1 = ((f32[32,1,64,128]{3,2,1,0:T(8,128)}), f32[32,1,64,128]{3,2,1,0:T(8,128)}, u32[]{:S(2)}, u32[]{:S(2)}) async-start(f32[32,1,64,128]{3,2,1,0:T(8,128)} %bitcast.34), calls=%async_computation.1 | async-start | bytes 2097152 | tf_op jit(solution)/shard_map/all_to_all | solution.py:38
  115.2 0.1 reshape.63
  115.4 0.1 reshape.71
  115.6 2.0 %gather_fusion = f32[64,64,64]{2,1,0:T(8,128)} fusion(f32[8,64,64]{2,1,0:T(8,128)S(1)} %copy-done.1, s32[1024]{0:T(1024)S(1)} %pad_clamp_fusion.4), kind=kCustom, calls=%fused_computation | custom fusion | bytes 2097408 | tf_op jit(solution)/shard_map/gather | solution.py:47
  117.6 2.0 %gather_fusion.1 = f32[64,64,128]{2,1,0:T(8,128)} fusion(f32[8,64,128]{2,1,0:T(8,128)S(1)} %copy-done.2, s32[1024]{0:T(1024)S(1)} %pad_clamp_fusion.3), kind=kCustom, calls=%fused_computation.1 | custom fusion | bytes 4194560 | tf_op jit(solution)/shard_map/gather | solution.py:48
  119.6 0.7 convert_reduce_fusion
  120.3 23.6 %all-to-all-done.1 = f32[32,1,64,128]{3,2,1,0:T(8,128)} async-done(((f32[32,1,64,128]{3,2,1,0:T(8,128)}), f32[32,1,64,128]{3,2,1,0:T(8,128)}, u32[]{:S(2)}, u32[]{:S(2)}) %all-to-all-start.1) | async-done | bytes 1048608 | tf_op jit(solution)/shard_map/all_to_all | solution.py:38
  143.9 0.1 broadcast_in_dim.21
  144.0 3.6 %scatter_fusion = f32[32,64,128]{2,1,0:T(8,128)S(1)} fusion(f32[32,64,128]{2,1,0:T(8,128)S(1)} %broadcast_in_dim.21, s32[32]{0:T(128)S(1)} %fusion.2, f32[32,64,128]{2,1,0:T(8,128)} %bitcast.13), kind=kCustom, calls=%fused_computation.6 | custom fusion | bytes 3145856 | tf_op jit(solution)/shard_map/scatter | solution.py:45
  147.6 5.5 %fusion = f32[32,64,128]{2,1,0:T(8,128)} fusion(f32[32,64,128]{2,1,0:T(8,128)S(1)} %scatter_fusion, f32[32,2,64,64]{3,2,1,0:T(8,128)} %bitcast.31, f32[32,2,64,128]{3,2,1,0:T(8,128)} %bitcast.32), kind=kOutput, calls=%fused_computation.9 | convolution fusion | flops 402915328 | bytes 5242880 | tf_op jit(solution)/shard_map/tmij,tmjk->tik/dot_general | solution.py:49
  (29 shorter events, 0.6 us)
Async XLA Ops:
  6.5 93.4 %copy-start = (f32[32,2,64,64]{3,2,1,0:T(8,128)S(1)}, f32[32,2,64,64]{3,2,1,0:T(8,128)}, u32[]{:S(2)}) copy-start(f32[32,2,64,64]{3,2,1,0:T(8,128)} %param.10) | copy-start | bytes 3145732
  6.5 89.2 %all-gather.2.cloned.1.call-start = ((), (), s32[]{:S(2)}) async-start(), calls=%async_computation.2 | async-start | bytes 4325376 | tf_op jit(solution)/shard_map/all_gather | solution.py:25
  11.6 93.6 %all-to-all-start = ((f32[32,1,1]{2,1,0:T(1,128)}), f32[32,1,1]{2,1,0:T(1,128)S(1)}, u32[]{:S(2)}, u32[]{:S(2)}) async-start(f32[32,1,1]{2,1,0:T(1,128)} %copy.23), calls=%async_computation | async-start | bytes 32768 | tf_op jit(solution)/shard_map/all_to_all | solution.py:39
  103.6 11.5 %copy-start.3 = (s32[32,2]{0,1:T(2,128)S(1)}, s32[32,2]{0,1:T(2,128)}, u32[]{:S(2)}) copy-start(s32[32,2]{0,1:T(2,128)} %param.16) | copy-start | bytes 772
  103.6 11.7 %copy-start.4 = (s32[32,2]{0,1:T(2,128)S(1)}, s32[32,2]{0,1:T(2,128)}, u32[]{:S(2)}) copy-start(s32[32,2]{0,1:T(2,128)} %param.17) | copy-start | bytes 772
  103.6 12.0 %copy-start.1 = (f32[8,64,64]{2,1,0:T(8,128)S(1)}, f32[8,64,64]{2,1,0:T(8,128)}, u32[]{:S(2)}) copy-start(f32[8,64,64]{2,1,0:T(8,128)} %param.14) | copy-start | bytes 393220
  105.2 38.7 %all-to-all-start.1 = ((f32[32,1,64,128]{3,2,1,0:T(8,128)}), f32[32,1,64,128]{3,2,1,0:T(8,128)}, u32[]{:S(2)}, u32[]{:S(2)}) async-start(f32[32,1,64,128]{3,2,1,0:T(8,128)} %bitcast.34), calls=%async_computation.1 | async-start | bytes 2097152 | tf_op jit(solution)/shard_map/all_to_all | solution.py:38
  115.6 2.1 %copy-start.2 = (f32[8,64,128]{2,1,0:T(8,128)S(1)}, f32[8,64,128]{2,1,0:T(8,128)}, u32[]{:S(2)}) copy-start(f32[8,64,128]{2,1,0:T(8,128)} %param.15) | copy-start | bytes 786436
Sparse Core Ops, SparseCore 0:
  10.1 85.5 all-gather.1
where the time goes:
time: 160 us
  waiting for transfers between devices  89.3 us (56%)
  starting transfers between devices  26.4 us (16%)
  local copies, waits for them, and re-layouts  16.5 us (10%)
  between operations  13.6 us (8%)
  matrix products  9.18 us (6%)
  other arithmetic  4.99 us (3%)
    all_gather x1, waiting for transfers between devices, body(): gathered = lax.all_gather(amp_cycle, 'col', axis=0, tiled=True)  65 us
    all_to_all x1, waiting for transfers between devices, body(): lax.all_to_all(outgoing, 'row', split_axis=0, concat_axis=0, tiled=True)  23.6 us
    all_to_all x1, starting transfers between devices, body(): lax.all_to_all(slot_index, 'row', split_axis=0, concat_axis=0, tiled=True)  16.5 us
    all_to_all x1, starting transfers between devices, body(): lax.all_to_all(outgoing, 'row', split_axis=0, concat_axis=0, tiled=True)  9.9 us
    dot_general x1, matrix products, body(): jnp.einsum('tmij,tmjk->tik', ladder_tiles, ladder_sources, precision=high...  5.5 us
    gather x3, local copies, waits for them, and re-layouts, body(): sources = gathered[lookup[cycle_refs]]  5.07 us
    dot_general x1, matrix products, body(): jnp.einsum('tsij,tsjk->tik', cycle_ints, sources, precision=highest)  3.67 us
    scatter x1, local copies, waits for them, and re-layouts, body(): cycle_here = jnp.zeros_like(cycle_part).at[placement].set(arrived.reshape...  3.58 us
  transfers between devices with their start and end apart: 3, of which 2 were waited for; matrix products, arithmetic and copies ran while one was open for 13% of the time, Pallas kernels for 0%

commit v1 on v0

v1 whole, which is shorter than its diff:
```python
import functools

import jax
import jax.numpy as jnp
from jax import lax
from jax.experimental import pallas as pl
from jax.experimental.pallas import tpu as pltpu
from jax.sharding import PartitionSpec as P

MESH = pl.DeviceIdType.MESH
NX, NY, NZ, NCORE = 4, 8, 16, 2
NQ = 4
NEAR = {1: 0, 2: 1, 3: 0, 4: 3, 5: 4, 6: 3, 7: 6, 8: 6}
RING = {m: m - 1 for m in range(1, 9)}
TREES = (NEAR, NEAR, RING, RING)
NEAR_AT = {1: 3.5, 3: 5.5, 2: 7.0, 4: 9.0, 6: 11.0, 5: 12.5, 7: 14.5, 8: 15.5}
RING_AT = {m: 3.6 * m for m in range(1, 9)}
START = (0.0, 0.01, 0.02, 0.03)
DELAY = (0.0, 6.0, 1.0, 2.0)
PIECE = 1.2
ORDER = (4, 3, 5, 2, 6, 1, 7, 0)


def shifted(value, blocks):
    amount = (blocks * 32) % 128
    return value if amount == 0 else pltpu.roll(value, amount, axis=1)


def pick(lane_block, choices):
    out = choices[0]
    for p in range(1, 4):
        out = jnp.where(lane_block == p, choices[p], out)
    return out


def split(value):
    high = value.astype(jnp.bfloat16)
    low = (value - high.astype(jnp.float32)).astype(jnp.bfloat16)
    return high, low


def kernel(
    amp_hbm,
    ints_hbm,
    refs_hbm,
    wanted_hbm,
    dest_hbm,
    lint_hbm,
    lamp_hbm,
    int_ref_hbm,
    amp_ref_hbm,
    out,
    refs,
    wanted,
    dest,
    int_ref,
    amp_ref,
    amp,
    ints,
    lint,
    lamp,
    held_0,
    held_1,
    held_2,
    held_3,
    lhs,
    going,
    came_0,
    came_1,
    came_2,
    came_3,
    passed,
    pair,
    dest_col,
    slot_row,
    slots,
    table,
    inverse,
    origin,
    place,
    which,
    load_sem,
    table_sem,
    ring_sem,
    ring_sent,
    twin_sem,
    relay_sem,
    slot_sem,
    slot_sent,
    row_sem,
    row_sent,
):
    came = (came_0, came_1, came_2, came_3)
    held = (held_0, held_1, held_2, held_3)
    row, col = lax.axis_index("row"), lax.axis_index("col")
    x, y = row // NY, row % NY
    z, core = col // NCORE, col % NCORE
    way = 1 - 2 * core
    mate = 1 - core

    def along(links, to_core):
        return (row, ((z + way * links + NZ) % NZ) * NCORE + to_core)

    twin = along(0, mate)

    def peer_row(k):
        return ((x + k % NX) % NX) * NY + (y + k // NX) % NY

    loads = [
        pltpu.make_async_copy(a, b, load_sem.at[i])
        for i, (a, b) in enumerate(
            (
                (amp_hbm, amp),
                (dest_hbm, dest),
                (refs_hbm, refs),
                (wanted_hbm, wanted),
                (ints_hbm, ints),
                (lint_hbm, lint),
                (lamp_hbm, lamp),
                (int_ref_hbm, int_ref),
                (amp_ref_hbm, amp_ref),
            )
        )
    ]
    for load in loads:
        load.start()

    barrier = pltpu.get_barrier_semaphore()
    senders = (
        along(-1, core),
        along(-2, core),
        along(-3, core),
        along(-1, mate),
        along(-3, mate),
        twin,
    )
    for device in senders:
        pl.semaphore_signal(barrier, inc=1, device_id=device, device_id_type=MESH)

    def greet(k, carry):
        pl.semaphore_signal(barrier, inc=1, device_id=(peer_row(k), col), device_id_type=MESH)
        return carry

    lax.fori_loop(1, 32, greet, 0)

    lane_block = lax.broadcasted_iota(jnp.int32, (16, 128), 1) // 32

    loads[0].wait()
    for w in range(4):
        skewed = [shifted(amp[w, 16 * a : 16 * a + 16, :], a) for a in range(4)]
        for q in range(NQ):
            held[q][core, w] = pick(lane_block, [skewed[(p - q) % 4] for p in range(4)])

    loads[1].wait()
    for t in range(32):
        dest_col[t : t + 1, :] = jnp.full((1, 128), dest[t], jnp.int32)
    lane = lax.broadcasted_iota(jnp.int32, (32, 128), 1)
    sub = lax.broadcasted_iota(jnp.int32, (32, 128), 0)
    goal = dest_col[...]
    to_row = (goal // 32) == lane
    table[0:1, :] = jnp.max(jnp.where(to_row, sub, 0), axis=0, keepdims=True)
    slot = jnp.max(jnp.where(to_row, goal % 32, 0), axis=0, keepdims=True)
    slot_row[...] = slot
    slots[0:1, :] = slot
    invert = pltpu.make_async_copy(table.at[0:1], inverse, table_sem)
    invert.start()

    pl.semaphore_wait(barrier, len(senders) + 31)

    def send(q, source, target, device, semaphore, sent=0):
        pltpu.make_async_remote_copy(
            src_ref=held[q].at[source],
            dst_ref=held[q].at[target],
            send_sem=ring_sent.at[q, sent],
            recv_sem=semaphore,
            device_id=device,
            device_id_type=MESH,
        ).start()

    def await_block(q, block, semaphore):
        ref = held[q].at[block]
        pltpu.make_async_copy(ref, ref, semaphore).wait()

    def blocks(first, last):
        return pl.ds(2 * first, 2 * (last - first))

    def onward(q, m):
        return sorted((n for n in TREES[q] if TREES[q][n] == m), reverse=True)

    def inject(q):
        for n in onward(q, 0):
            send(q, core, 2 * n + core, along(n, core), ring_sem.at[q, n, core])
            send(q, core, 2 * n + core, along(-n, mate), ring_sem.at[q, n, core])
        send(q, core, core, twin, twin_sem.at[q, 0], sent=1)

    def hop(q, m):
        if TREES[q][m] == 0:
            for c in range(NCORE):
                await_block(q, 2 * m + c, ring_sem.at[q, m, c])
        elif m < 8:
            await_block(q, blocks(m, m + 1), ring_sem.at[q, m, 0])
        else:
            await_block(q, 16 + core, ring_sem.at[q, 8, 0])
        for n in onward(q, m):
            if n == 8:
                send(q, 2 * m + core, 16 + core, along(8 - m, core), ring_sem.at[q, 8, 0])
            else:
                send(q, blocks(m, m + 1), blocks(n, n + 1), along(n - m, core), ring_sem.at[q, n, 0])
        if m == 8:
            send(q, 16 + core, 34 + core, twin, twin_sem.at[q, 2], sent=3)
        else:
            send(q, blocks(m, m + 1), blocks(m + 9, m + 10), twin, twin_sem.at[q, 1], sent=2)

    def others(q):
        await_block(q, mate, twin_sem.at[q, 0])
        await_block(q, blocks(10, 17), twin_sem.at[q, 1])
        await_block(q, 34 + mate, twin_sem.at[q, 2])

    def send_slots():
        def one(k, carry):
            pltpu.make_async_remote_copy(
                src_ref=slot_row,
                dst_ref=slots.at[pl.ds(k, 1)],
                send_sem=slot_sent,
                recv_sem=slot_sem,
                device_id=(peer_row(k), col),
                device_id_type=MESH,
            ).start()
            return carry

        lax.fori_loop(1, 32, one, 0)

    def indices():
        invert.wait()
        loads[2].wait()
        loads[3].wait()

        def one(k, carry):
            t = inverse[0, peer_row(k)]
            for s in range(2):
                h = refs[s, t]
                m = (way * (z - h // 2) + 2 * NZ) % NZ
                own = jnp.logical_or(m < 8, jnp.logical_and(m == 8, h % 2 == core))
                place[2 * k + s] = jnp.where(own, 2 * m, 18 + 2 * (NZ - m)) + h % 2
                which[2 * k + s] = wanted[0, h]
            return carry

        lax.fori_loop(0, 32, one, 0, unroll=4)

    def prepare_ints():
        loads[4].wait()

        def one(k, carry):
            t = inverse[0, peer_row(k)]
            both = jnp.concatenate([ints[t, 0], ints[t, 1]], axis=1)
            high, low = split(both)
            lhs[k] = jnp.concatenate([high, low], axis=1)
            return carry

        lax.fori_loop(0, 32, one, 0, unroll=4)

    def ladder_pairs():
        loads[5].wait()
        loads[6].wait()
        ih, il = split(lint[...].reshape(512, 64))
        left = jnp.concatenate([ih, il, ih], axis=1)

        def one(b, carry):
            high, low = split(lamp[b])
            right = jnp.concatenate([high, high, low], axis=0)
            product = jnp.dot(left, right, preferred_element_type=jnp.float32)
            pair[b] = product.reshape(8, 64, 128)
            return carry

        lax.fori_loop(0, 8, one, 0, unroll=2)

    def arrivals():
        pltpu.make_async_copy(slots.at[1:32], slots.at[1:32], slot_sem).wait()
        mine = jnp.max(jnp.where(lane == row, slots[...], 0), axis=1, keepdims=True)
        table[1:2, :] = jnp.max(jnp.where(mine == lane, sub, 0), axis=0, keepdims=True)
        copy = pltpu.make_async_copy(table.at[1:2], origin, table_sem)
        copy.start()
        copy.wait()

    def chunk_products(q, i):
        rows = []
        for s in range(2):
            turned = [
                shifted(held[q][place[8 * i + 2 * e + s], which[8 * i + 2 * e + s]], e)
                for e in range(4)
            ]
            for a in range(4):
                mixed = pick(lane_block, [turned[(p - a - q) % 4] for p in range(4)])
                rows.append(shifted(mixed, -a - q))
        high, low = split(jnp.concatenate(rows, axis=0))
        left = lhs[pl.ds(4 * i, 4)].reshape(256, 256)
        product = jnp.dot(
            left, jnp.concatenate([high, high], axis=0), preferred_element_type=jnp.float32
        ) + jnp.dot(left[:, :128], low, preferred_element_type=jnp.float32)
        for e in range(4):
            parts = [
                shifted(product[64 * e + 16 * a : 64 * e + 16 * a + 16, :], a) for a in range(4)
            ]
            mixed = pick(lane_block, [parts[(p - e) % 4] for p in range(4)])
            going[4 * i + e, q] = shifted(mixed, q - e)

    def row_send(q, k):
        pltpu.make_async_remote_copy(
            src_ref=going.at[k, q],
            dst_ref=came[q].at[k],
            send_sem=row_sent.at[q],
            recv_sem=row_sem.at[q],
            device_id=(peer_row(k), col),
            device_id_type=MESH,
        ).start()

    def relay_copy(q):
        return pltpu.make_async_remote_copy(
            src_ref=going.at[16:20, q],
            dst_ref=passed.at[q],
            send_sem=relay_sem.at[q, 0],
            recv_sem=relay_sem.at[q, 1],
            device_id=(x * NY + (y + NY - 1) % NY, col),
            device_id_type=MESH,
        )

    def relay(q):
        @pl.when(core == 1)
        def _():
            relay_copy(q).wait_recv()
            for dx in range(NX):
                pltpu.make_async_remote_copy(
                    src_ref=passed.at[q, dx],
                    dst_ref=came[q].at[16 + dx],
                    send_sem=relay_sem.at[q, 2],
                    recv_sem=row_sem.at[q],
                    device_id=(peer_row(20 + dx), col),
                    device_id_type=MESH,
                ).start()

    def products(q, piece):
        for i in ORDER[2 * piece : 2 * piece + 2]:
            chunk_products(q, i)
        for i in ORDER[2 * piece : 2 * piece + 2]:
            if i == 4:

                @pl.when(core == 0)
                def _():
                    for e in range(4):
                        row_send(q, 16 + e)

                @pl.when(core == 1)
                def _():
                    relay_copy(q).start()

            else:
                for e in range(4):
                    if i + e > 0:
                        row_send(q, 4 * i + e)
        if piece == 3:
            came[q][0] = going[0, q]

    def row_wait(q):
        block = came[q].at[1:32]
        pltpu.make_async_copy(block, block, row_sem.at[q]).wait()

    def ladder():
        loads[7].wait()
        loads[8].wait()

        def one(u, carry):
            first = pair[amp_ref[0, u], int_ref[0, u]]
            out[u] = first + pair[amp_ref[1, u], int_ref[1, u]]
            return carry

        lax.fori_loop(0, 32, one, 0, unroll=4)

    def finish(chunks):
        for q in chunks:
            row_wait(q)

        def one(u, carry):
            k = origin[0, u]
            tiles = {q: came[q][k] for q in chunks}
            for a in range(4):
                rows = slice(16 * a, 16 * a + 16)
                mixed = jnp.zeros((16, 128), jnp.float32)
                for q in chunks:
                    mixed = jnp.where(lane_block == (a + q) % 4, tiles[q], mixed)
                out[u, rows, :] += shifted(mixed, -a)
            return carry

        lax.fori_loop(0, 32, one, 0, unroll=4)

    tasks = []
    ready = []
    for q in range(NQ):
        tasks.append((START[q], functools.partial(inject, q)))
        at = {m: START[q] + DELAY[q] + t for m, t in (RING_AT if TREES[q] is RING else NEAR_AT).items()}
        for m, t in at.items():
            tasks.append((t, functools.partial(hop, q, m)))
        ready.append(max([max(at.values()) + 1.0] + [t + 4 * PIECE for t in ready]))
        tasks.append((ready[q], functools.partial(others, q)))
        for piece in range(4):
            tasks.append((ready[q] + PIECE * piece, functools.partial(products, q, piece)))
        tasks.append((ready[q] + 3.0 * PIECE + 0.1, functools.partial(relay, q)))
    tasks += [
        (0.2, send_slots),
        (1.0, indices),
        (3.51, prepare_ints),
        (5.51, ladder_pairs),
        (7.01, ladder),
        (9.01, arrivals),
        (ready[3] + 4 * PIECE, functools.partial(finish, (0, 1, 2))),
        (ready[3] + 5 * PIECE, functools.partial(finish, (3,))),
    ]
    for _, task in sorted(tasks, key=lambda entry: entry[0]):
        task()

    for q in range(NQ):
        sends = 2 * len(onward(q, 0)) + 2 * sum(0 < TREES[q][n] and n < 8 for n in TREES[q]) + 1
        await_block(q, pl.ds(0, sends), ring_sent.at[q, 0])
        await_block(q, core, ring_sent.at[q, 1])
        await_block(q, blocks(1, 8), ring_sent.at[q, 2])
        await_block(q, 16 + core, ring_sent.at[q, 3])

        @pl.when(core == 0)
        def _():
            block = going.at[1:32, q]
            pltpu.make_async_copy(block, block, row_sent.at[q]).wait()

        @pl.when(core == 1)
        def _():
            relay_copy(q).wait_send()
            pltpu.make_async_copy(passed.at[q], passed.at[q], relay_sem.at[q, 2]).wait()
            block = going.at[1:28, q]
            pltpu.make_async_copy(block, block, row_sent.at[q]).wait()

    pltpu.make_async_copy(slots.at[1:32], slots.at[1:32], slot_sent).wait()


def body(
    amp_cycle,
    cycle_ints,
    cycle_refs,
    wanted,
    cycle_dest,
    ladder_ints,
    ladder_amps,
    ladder_int_ref,
    ladder_amp_ref,
):
    operands = (
        amp_cycle,
        cycle_ints,
        cycle_refs.T,
        wanted.reshape(1, 32),
        cycle_dest,
        ladder_ints,
        ladder_amps,
        ladder_int_ref.T,
        ladder_amp_ref.T,
    )
    f32, i32 = jnp.float32, jnp.int32
    hbm = pl.BlockSpec(memory_space=pltpu.HBM)
    dma = pltpu.SemaphoreType.DMA
    return pl.pallas_call(
        kernel,
        out_shape=jax.ShapeDtypeStruct((32, 64, 128), f32),
        in_specs=[hbm] * 9,
        out_specs=pl.BlockSpec(memory_space=pltpu.VMEM),
        scratch_shapes=[
            pltpu.SMEM((2, 32), i32),
            pltpu.SMEM((1, 32), i32),
            pltpu.SMEM((32,), i32),
            pltpu.SMEM((2, 32), i32),
            pltpu.SMEM((2, 32), i32),
            pltpu.VMEM((4, 64, 128), f32),
            pltpu.VMEM((32, 2, 64, 64), f32),
            pltpu.VMEM((8, 64, 64), f32),
            pltpu.VMEM((8, 64, 128), f32),
            *[pltpu.VMEM((36, 4, 16, 128), f32)] * NQ,
            pltpu.VMEM((32, 64, 256), jnp.bfloat16),
            pltpu.VMEM((32, NQ, 16, 128), f32),
            *[pltpu.VMEM((32, 16, 128), f32)] * NQ,
            pltpu.VMEM((NQ, NX, 16, 128), f32),
            pltpu.VMEM((8, 8, 64, 128), f32),
            pltpu.VMEM((32, 128), i32),
            pltpu.VMEM((1, 128), i32),
            pltpu.VMEM((32, 128), i32),
            pltpu.VMEM((8, 128), i32),
            pltpu.SMEM((1, 128), i32),
            pltpu.SMEM((1, 128), i32),
            pltpu.SMEM((64,), i32),
            pltpu.SMEM((64,), i32),
            dma((9,)),
            dma,
            dma((NQ, 9, 2)),
            dma((NQ, 4)),
            dma((NQ, 3)),
            dma((NQ, 3)),
            dma,
            dma,
            dma((NQ,)),
            dma((NQ,)),
        ],
        compiler_params=pltpu.CompilerParams(
            collective_id=0, has_side_effects=True, vmem_limit_bytes=62 << 20
        ),
        name="cycle_and_ladder",
    )(*operands)


def solution(mesh):
    both = ("row", "col")
    placed = (
        P(both, None, None),
        P(both, None, None, None),
        P(both, None),
        P(both, None, None),
        P(both),
        P(both, None, None),
        P(both, None, None),
        P(both, None),
        P(both, None),
    )
    return jax.shard_map(
        body, mesh=mesh, in_specs=placed, out_specs=P(both, None, None), check_vma=False
    )
```

time: 160 us -> 83.6 us (0.52)
  the two profiles are of different devices: /device:TPU:8 before, /device:TPU:1 now
where the time goes in v1:
time: 83.6 us; the launch traced here: 83.5 us
  Pallas kernels  81.1 us (97%)
  local copies, waits for them, and re-layouts  2.31 us (3%)
    pallas_call x1, Pallas kernels, body(): pl.pallas_call(kernel, out_shape=jax.ShapeDtypeStruct((32, 64, 128), f32)...  81.1 us
    unnamed x1, local copies, waits for them, and re-layouts  2.31 us

profile of v1, /device:TPU:1, one launch (start us, length us, event | category | flops | bytes accessed | tf_op | source)
XLA Modules:
  0.0 83.5 jit_solution(18436419501548280058)
XLA Ops:
  0.0 81.1 %cycle_and_ladder.1 = f32[32,64,128]{2,1,0:T(8,128)} custom-call(f32[4,64,128]{2,1,0:T(8,128)} %amp_hbm.1, f32[32,2,64,64]{3,2,1,0:T(8,128)} %ints_hbm.1, s32[2,32]{1,0:T(2,128)} %bitcast.4, s32[1,32]{1,0:T(1,128)} %bitcast.7, s32[32]{0:T(128)} %dest_hbm.1, f32[8,64,64]{2,1,0:T(8,128)} %lint_hbm.1, f32[8,64,128]{2,1,0:T(8,128)} %lamp_hbm.1, ...), custom_call_target="tpu_custom_call" | custom-call | tf_op jit(solution)/shard_map/cycle_and_ladder/pallas_call | solution.py:467
  81.2 2.3 %copy.11 = f32[32,64,128]{2,1,0:T(8,128)} copy(f32[32,64,128]{2,1,0:T(8,128)} %cycle_and_ladder.1) | data formatting | bytes 2097152

commit v2 on v1

--- a/solution.py
+++ b/solution.py
@@ -10,14 +10,28 @@
 MESH = pl.DeviceIdType.MESH
 NX, NY, NZ, NCORE = 4, 8, 16, 2
 NQ = 4
-NEAR = {1: 0, 2: 1, 3: 0, 4: 3, 5: 4, 6: 3, 7: 6, 8: 6}
-RING = {m: m - 1 for m in range(1, 9)}
-TREES = (NEAR, NEAR, RING, RING)
-NEAR_AT = {1: 3.5, 3: 5.5, 2: 7.0, 4: 9.0, 6: 11.0, 5: 12.5, 7: 14.5, 8: 15.5}
-RING_AT = {m: 3.6 * m for m in range(1, 9)}
-START = (0.0, 0.01, 0.02, 0.03)
-DELAY = (0.0, 6.0, 1.0, 2.0)
-PIECE = 1.2
+TREES = (
+    {1: 0, 2: 1, 3: 0, 4: 3, 5: 4, 6: 3, 7: 6, 8: 6},
+    {1: 0, 2: 1, 3: 2, 4: 0, 5: 4, 6: 5, 7: 6, 8: 7},
+    {1: 0, 2: 1, 3: 2, 4: 3, 5: 4, 6: 5, 7: 6, 8: 7},
+    {1: 0, 2: 1, 3: 0, 4: 3, 5: 4, 6: 3, 7: 6, 8: 6},
+)
+
+(INJECT, HOP, GATHERED, MULTIPLY, SLOTS, INDICES, INTS, PAIRS, LADDER, ORIGINS, FINISH) = range(11)
+STEPS = (
+    (INJECT, 0), (INJECT, 2), (SLOTS,), (INJECT, 1), (INDICES,), (INTS,), (HOP, 0, 1),
+    (HOP, 2, 1), (PAIRS,), (HOP, 1, 1), (HOP, 0, 3), (LADDER,), (ORIGINS,), (HOP, 0, 2),
+    (HOP, 2, 2), (HOP, 1, 4), (HOP, 1, 2), (HOP, 0, 4), (HOP, 2, 3), (HOP, 1, 5), (HOP, 0, 6),
+    (HOP, 1, 3), (HOP, 0, 5), (HOP, 2, 4), (HOP, 1, 6), (INJECT, 3), (HOP, 0, 7), (HOP, 0, 8),
+    (HOP, 2, 5), (GATHERED, 0), (MULTIPLY, 0, 0), (HOP, 1, 7), (MULTIPLY, 0, 1),
+    (MULTIPLY, 0, 2), (HOP, 3, 1), (MULTIPLY, 0, 3), (HOP, 2, 6), (HOP, 3, 3), (HOP, 1, 8),
+    (HOP, 3, 2), (GATHERED, 1), (MULTIPLY, 1, 0), (HOP, 2, 7), (MULTIPLY, 1, 1),
+    (MULTIPLY, 1, 2), (HOP, 3, 4), (MULTIPLY, 1, 3), (HOP, 3, 6), (HOP, 2, 8), (GATHERED, 2),
+    (MULTIPLY, 2, 0), (HOP, 3, 5), (MULTIPLY, 2, 1), (MULTIPLY, 2, 2), (HOP, 3, 7), (HOP, 3, 8),
+    (MULTIPLY, 2, 3), (GATHERED, 3), (MULTIPLY, 3, 0), (MULTIPLY, 3, 1), (MULTIPLY, 3, 2),
+    (MULTIPLY, 3, 3), (FINISH, (0, 1, 2)), (FINISH, (3,)),
+)
+
 ORDER = (4, 3, 5, 2, 6, 1, 7, 0)
 
 
@@ -69,7 +83,6 @@
     came_1,
     came_2,
     came_3,
-    passed,
     pair,
     dest_col,
     slot_row,
@@ -84,7 +97,6 @@
     ring_sem,
     ring_sent,
     twin_sem,
-    relay_sem,
     slot_sem,
     slot_sent,
     row_sem,
@@ -126,22 +138,24 @@
         load.start()
 
     barrier = pltpu.get_barrier_semaphore()
-    senders = (
-        along(-1, core),
-        along(-2, core),
-        along(-3, core),
-        along(-1, mate),
-        along(-3, mate),
-        twin,
-    )
+    def greet(device):
+        pl.semaphore_signal(barrier, inc=1, device_id=device, device_id_type=MESH)
+
+    def greet_rows(first, last):
+        def one(k, carry):
+            greet((peer_row((k + 16) % 32), col))
+            return carry
+
+        lax.fori_loop(first, last, one, 0)
+
+    starts = sorted({n for tree in TREES for n in tree if tree[n] == 0})
+    strides = sorted({n - tree[n] for tree in TREES for n in tree})
+    senders = [along(-links, core) for links in strides]
+    senders += [along(-links, mate) for links in starts] + [twin]
+    greet_rows(0, 16)
     for device in senders:
-        pl.semaphore_signal(barrier, inc=1, device_id=device, device_id_type=MESH)
-
-    def greet(k, carry):
-        pl.semaphore_signal(barrier, inc=1, device_id=(peer_row(k), col), device_id_type=MESH)
-        return carry
-
-    lax.fori_loop(1, 32, greet, 0)
+        greet(device)
+    greet_rows(17, 32)
 
     lane_block = lax.broadcasted_iota(jnp.int32, (16, 128), 1) // 32
 
@@ -314,49 +328,13 @@
             device_id_type=MESH,
         ).start()
 
-    def relay_copy(q):
-        return pltpu.make_async_remote_copy(
-            src_ref=going.at[16:20, q],
-            dst_ref=passed.at[q],
-            send_sem=relay_sem.at[q, 0],
-            recv_sem=relay_sem.at[q, 1],
-            device_id=(x * NY + (y + NY - 1) % NY, col),
-            device_id_type=MESH,
-        )
-
-    def relay(q):
-        @pl.when(core == 1)
-        def _():
-            relay_copy(q).wait_recv()
-            for dx in range(NX):
-                pltpu.make_async_remote_copy(
-                    src_ref=passed.at[q, dx],
-                    dst_ref=came[q].at[16 + dx],
-                    send_sem=relay_sem.at[q, 2],
-                    recv_sem=row_sem.at[q],
-                    device_id=(peer_row(20 + dx), col),
-                    device_id_type=MESH,
-                ).start()
-
     def products(q, piece):
         for i in ORDER[2 * piece : 2 * piece + 2]:
             chunk_products(q, i)
         for i in ORDER[2 * piece : 2 * piece + 2]:
-            if i == 4:
-
-                @pl.when(core == 0)
-                def _():
-                    for e in range(4):
-                        row_send(q, 16 + e)
-
-                @pl.when(core == 1)
-                def _():
-                    relay_copy(q).start()
-
-            else:
-                for e in range(4):
-                    if i + e > 0:
-                        row_send(q, 4 * i + e)
+            for e in range(4):
+                if i + e > 0:
+                    row_send(q, 4 * i + e)
         if piece == 3:
             came[q][0] = going[0, q]
 
@@ -392,30 +370,21 @@
 
         lax.fori_loop(0, 32, one, 0, unroll=4)
 
-    tasks = []
-    ready = []
-    for q in range(NQ):
-        tasks.append((START[q], functools.partial(inject, q)))
-        at = {m: START[q] + DELAY[q] + t for m, t in (RING_AT if TREES[q] is RING else NEAR_AT).items()}
-        for m, t in at.items():
-            tasks.append((t, functools.partial(hop, q, m)))
-        ready.append(max([max(at.values()) + 1.0] + [t + 4 * PIECE for t in ready]))
-        tasks.append((ready[q], functools.partial(others, q)))
-        for piece in range(4):
-            tasks.append((ready[q] + PIECE * piece, functools.partial(products, q, piece)))
-        tasks.append((ready[q] + 3.0 * PIECE + 0.1, functools.partial(relay, q)))
-    tasks += [
-        (0.2, send_slots),
-        (1.0, indices),
-        (3.51, prepare_ints),
-        (5.51, ladder_pairs),
-        (7.01, ladder),
-        (9.01, arrivals),
-        (ready[3] + 4 * PIECE, functools.partial(finish, (0, 1, 2))),
-        (ready[3] + 5 * PIECE, functools.partial(finish, (3,))),
-    ]
-    for _, task in sorted(tasks, key=lambda entry: entry[0]):
-        task()
+    acts = {
+        INJECT: inject,
+        HOP: hop,
+        GATHERED: others,
+        MULTIPLY: products,
+        SLOTS: send_slots,
+        INDICES: indices,
+        INTS: prepare_ints,
+        PAIRS: ladder_pairs,
+        LADDER: ladder,
+        ORIGINS: arrivals,
+        FINISH: lambda *chunks: finish(chunks[0]),
+    }
+    for act, *details in STEPS:
+        acts[act](*details)
 
     for q in range(NQ):
         sends = 2 * len(onward(q, 0)) + 2 * sum(0 < TREES[q][n] and n < 8 for n in TREES[q]) + 1
@@ -424,17 +393,8 @@
         await_block(q, blocks(1, 8), ring_sent.at[q, 2])
         await_block(q, 16 + core, ring_sent.at[q, 3])
 
-        @pl.when(core == 0)
-        def _():
-            block = going.at[1:32, q]
-            pltpu.make_async_copy(block, block, row_sent.at[q]).wait()
-
-        @pl.when(core == 1)
-        def _():
-            relay_copy(q).wait_send()
-            pltpu.make_async_copy(passed.at[q], passed.at[q], relay_sem.at[q, 2]).wait()
-            block = going.at[1:28, q]
-            pltpu.make_async_copy(block, block, row_sent.at[q]).wait()
+        block = going.at[1:32, q]
+        pltpu.make_async_copy(block, block, row_sent.at[q]).wait()
 
     pltpu.make_async_copy(slots.at[1:32], slots.at[1:32], slot_sent).wait()
 
@@ -483,7 +443,6 @@
             pltpu.VMEM((32, 64, 256), jnp.bfloat16),
             pltpu.VMEM((32, NQ, 16, 128), f32),
             *[pltpu.VMEM((32, 16, 128), f32)] * NQ,
-            pltpu.VMEM((NQ, NX, 16, 128), f32),
             pltpu.VMEM((8, 8, 64, 128), f32),
             pltpu.VMEM((32, 128), i32),
             pltpu.VMEM((1, 128), i32),
@@ -498,17 +457,16 @@
             dma((NQ, 9, 2)),
             dma((NQ, 4)),
             dma((NQ, 3)),
-            dma((NQ, 3)),
             dma,
             dma,
             dma((NQ,)),
             dma((NQ,)),
         ],
         compiler_params=pltpu.CompilerParams(
-            collective_id=0, has_side_effects=True, vmem_limit_bytes=62 << 20
+            collective_id=0, has_side_effects=True, vmem_limit_bytes=40 << 20
         ),
         name="cycle_and_ladder",
-    )(*operands)
+    )(*(pltpu.with_memory_space_constraint(v, pltpu.HBM) for v in operands))
 
 
 def solution(mesh):

time: 83.6 us -> 76.7 us (0.917)
  Pallas kernels: 81.1 us -> 75.6 us
  local copies, waits for them, and re-layouts: 2.31 us -> 0.97 us
    pallas_call x1, Pallas kernels: 81.1 us -> 75.6 us  [body(): pl.pallas_call(kernel, out_shape=jax.ShapeDtypeStruct((32, 64, 128), f32)...]
    unnamed x1, local copies, waits for them, and re-layouts: 2.31 us -> 0.97 us
where the time goes in v2:
time: 76.7 us; the launch traced here: 76.5 us
  Pallas kernels  75.6 us (99%)
  local copies, waits for them, and re-layouts  0.97 us (1%)
    pallas_call x1, Pallas kernels, body(): pl.pallas_call(kernel, out_shape=jax.ShapeDtypeStruct((32, 64, 128), f32)...  75.6 us

profile of v2, /device:TPU:1, one launch (start us, length us, event | category | flops | bytes accessed | tf_op | source)
XLA Modules:
  0.0 76.5 jit_solution(13415215427742039768)
XLA Ops:
  0.0 75.6 %cycle_and_ladder.1 = f32[32,64,128]{2,1,0:T(8,128)S(1)} custom-call(f32[4,64,128]{2,1,0:T(8,128)} %amp_hbm.1, f32[32,2,64,64]{3,2,1,0:T(8,128)} %ints_hbm.1, s32[2,32]{1,0:T(2,128)} %bitcast.4, s32[1,32]{1,0:T(1,128)} %bitcast.7, s32[32]{0:T(128)} %dest_hbm.1, f32[8,64,64]{2,1,0:T(8,128)} %lint_hbm.1, f32[8,64,128]{2,1,0:T(8,128)} %lamp_hbm.1, ...), custom_call_target="tpu_custom_call" | custom-call | tf_op jit(solution)/shard_map/cycle_and_ladder/pallas_call | solution.py:427
  75.6 1.0 %copy.11 = f32[32,64,128]{2,1,0:T(8,128)} copy(f32[32,64,128]{2,1,0:T(8,128)S(1)} %cycle_and_ladder.1) | data formatting | bytes 2097152

commit v3 on v2

--- a/solution.py
+++ b/solution.py
@@ -11,25 +11,26 @@
 NX, NY, NZ, NCORE = 4, 8, 16, 2
 NQ = 4
 TREES = (
-    {1: 0, 2: 1, 3: 0, 4: 3, 5: 4, 6: 3, 7: 6, 8: 6},
-    {1: 0, 2: 1, 3: 2, 4: 0, 5: 4, 6: 5, 7: 6, 8: 7},
     {1: 0, 2: 1, 3: 2, 4: 3, 5: 4, 6: 5, 7: 6, 8: 7},
+    {1: 0, 2: 0, 3: 2, 4: 2, 5: 4, 6: 4, 7: 6, 8: 6},
+    {1: 0, 2: 0, 3: 2, 4: 2, 5: 4, 6: 4, 7: 6, 8: 6},
     {1: 0, 2: 1, 3: 0, 4: 3, 5: 4, 6: 3, 7: 6, 8: 6},
 )
 
 (INJECT, HOP, GATHERED, MULTIPLY, SLOTS, INDICES, INTS, PAIRS, LADDER, ORIGINS, FINISH) = range(11)
 STEPS = (
-    (INJECT, 0), (INJECT, 2), (SLOTS,), (INJECT, 1), (INDICES,), (INTS,), (HOP, 0, 1),
-    (HOP, 2, 1), (PAIRS,), (HOP, 1, 1), (HOP, 0, 3), (LADDER,), (ORIGINS,), (HOP, 0, 2),
-    (HOP, 2, 2), (HOP, 1, 4), (HOP, 1, 2), (HOP, 0, 4), (HOP, 2, 3), (HOP, 1, 5), (HOP, 0, 6),
-    (HOP, 1, 3), (HOP, 0, 5), (HOP, 2, 4), (HOP, 1, 6), (INJECT, 3), (HOP, 0, 7), (HOP, 0, 8),
-    (HOP, 2, 5), (GATHERED, 0), (MULTIPLY, 0, 0), (HOP, 1, 7), (MULTIPLY, 0, 1),
-    (MULTIPLY, 0, 2), (HOP, 3, 1), (MULTIPLY, 0, 3), (HOP, 2, 6), (HOP, 3, 3), (HOP, 1, 8),
-    (HOP, 3, 2), (GATHERED, 1), (MULTIPLY, 1, 0), (HOP, 2, 7), (MULTIPLY, 1, 1),
-    (MULTIPLY, 1, 2), (HOP, 3, 4), (MULTIPLY, 1, 3), (HOP, 3, 6), (HOP, 2, 8), (GATHERED, 2),
-    (MULTIPLY, 2, 0), (HOP, 3, 5), (MULTIPLY, 2, 1), (MULTIPLY, 2, 2), (HOP, 3, 7), (HOP, 3, 8),
-    (MULTIPLY, 2, 3), (GATHERED, 3), (MULTIPLY, 3, 0), (MULTIPLY, 3, 1), (MULTIPLY, 3, 2),
-    (MULTIPLY, 3, 3), (FINISH, (0, 1, 2)), (FINISH, (3,)),
+    (INJECT, 0), (INJECT, 2), (INDICES,), (INJECT, 1), (INTS, 0), (INTS, 1), (INTS, 2),
+    (HOP, 0, 1), (INTS, 3), (INTS, 4), (INTS, 5), (HOP, 2, 1), (INTS, 6), (HOP, 2, 2),
+    (INTS, 7), (SLOTS, 0), (HOP, 1, 1), (SLOTS, 1), (HOP, 0, 2), (HOP, 1, 2), (SLOTS, 2),
+    (SLOTS, 3), (HOP, 2, 3), (HOP, 2, 4), (HOP, 0, 3), (HOP, 1, 3), (HOP, 1, 4), (HOP, 2, 5),
+    (HOP, 0, 4), (HOP, 2, 6), (HOP, 1, 5), (INJECT, 3), (HOP, 1, 6), (HOP, 0, 5), (HOP, 2, 7),
+    (HOP, 2, 8), (GATHERED, 2), (MULTIPLY, 2, 0), (HOP, 3, 1), (MULTIPLY, 2, 1), (HOP, 1, 7),
+    (MULTIPLY, 2, 2), (HOP, 0, 6), (HOP, 1, 8), (MULTIPLY, 2, 3), (HOP, 3, 3), (HOP, 3, 2),
+    (GATHERED, 1), (MULTIPLY, 1, 0), (MULTIPLY, 1, 1), (HOP, 0, 7), (MULTIPLY, 1, 2),
+    (MULTIPLY, 1, 3), (HOP, 3, 4), (HOP, 3, 6), (HOP, 0, 8), (GATHERED, 0), (MULTIPLY, 0, 0),
+    (HOP, 3, 5), (MULTIPLY, 0, 1), (MULTIPLY, 0, 2), (HOP, 3, 7), (HOP, 3, 8), (MULTIPLY, 0, 3),
+    (GATHERED, 3), (MULTIPLY, 3, 0), (MULTIPLY, 3, 1), (MULTIPLY, 3, 2), (MULTIPLY, 3, 3),
+    (PAIRS,), (LADDER,), (ORIGINS,), (FINISH, (0, 1, 2)), (FINISH, (3,)),
 )
 
 ORDER = (4, 3, 5, 2, 6, 1, 7, 0)
@@ -230,8 +231,8 @@
         await_block(q, blocks(10, 17), twin_sem.at[q, 1])
         await_block(q, 34 + mate, twin_sem.at[q, 2])
 
-    def send_slots():
-        def one(k, carry):
+    def send_slots(part):
+        for k in range(max(1, 8 * part), 8 * part + 8):
             pltpu.make_async_remote_copy(
                 src_ref=slot_row,
                 dst_ref=slots.at[pl.ds(k, 1)],
@@ -240,9 +241,6 @@
                 device_id=(peer_row(k), col),
                 device_id_type=MESH,
             ).start()
-            return carry
-
-        lax.fori_loop(1, 32, one, 0)
 
     def indices():
         invert.wait()
@@ -261,17 +259,14 @@
 
         lax.fori_loop(0, 32, one, 0, unroll=4)
 
-    def prepare_ints():
-        loads[4].wait()
-
-        def one(k, carry):
+    def prepare_ints(part):
+        if part == 0:
+            loads[4].wait()
+        for k in range(4 * part, 4 * part + 4):
             t = inverse[0, peer_row(k)]
             both = jnp.concatenate([ints[t, 0], ints[t, 1]], axis=1)
             high, low = split(both)
             lhs[k] = jnp.concatenate([high, low], axis=1)
-            return carry
-
-        lax.fori_loop(0, 32, one, 0, unroll=4)
 
     def ladder_pairs():
         loads[5].wait()

time: 76.7 us -> 75.7 us (0.987)
  Pallas kernels: 75.6 us -> 74.6 us
    pallas_call x1, Pallas kernels: 75.6 us -> 74.6 us  [body(): pl.pallas_call(kernel, out_shape=jax.ShapeDtypeStruct((32, 64, 128), f32)...]
where the time goes in v3:
time: 75.7 us; the launch traced here: 75.6 us
  Pallas kernels  74.6 us (99%)
  local copies, waits for them, and re-layouts  0.97 us (1%)
    pallas_call x1, Pallas kernels, body(): pl.pallas_call(kernel, out_shape=jax.ShapeDtypeStruct((32, 64, 128), f32)...  74.6 us

profile of v3, /device:TPU:1, one launch (start us, length us, event | category | flops | bytes accessed | tf_op | source)
XLA Modules:
  0.0 75.6 jit_solution(13098823168076243600)
XLA Ops:
  0.0 74.6 %cycle_and_ladder.1 = f32[32,64,128]{2,1,0:T(8,128)S(1)} custom-call(f32[4,64,128]{2,1,0:T(8,128)} %amp_hbm.1, f32[32,2,64,64]{3,2,1,0:T(8,128)} %ints_hbm.1, s32[2,32]{1,0:T(2,128)} %bitcast.4, s32[1,32]{1,0:T(1,128)} %bitcast.7, s32[32]{0:T(128)} %dest_hbm.1, f32[8,64,64]{2,1,0:T(8,128)} %lint_hbm.1, f32[8,64,128]{2,1,0:T(8,128)} %lamp_hbm.1, ...), custom_call_target="tpu_custom_call" | custom-call | tf_op jit(solution)/shard_map/cycle_and_ladder/pallas_call | solution.py:422
  74.6 1.0 %copy.11 = f32[32,64,128]{2,1,0:T(8,128)} copy(f32[32,64,128]{2,1,0:T(8,128)S(1)} %cycle_and_ladder.1) | data formatting | bytes 2097152
